TPU v7x, 512 devices: a whole 4x4x16 slice. The times are simulated.
512 devices in a mesh: segment: 4 (over y_lo, core), ctx: 32 (over z, y_hi), head: 4 (over x).
Axes of the slice: x: 4, y: 4 (y_hi: 2, y_lo: 2; y = y_hi * 2 + y_lo), z: 16, core: 2. Of those that a mesh axis runs over, the one named last changes fastest.
Arguments:
- hidden: bfloat16 [4, 8192, 2880], P('segment', 'ctx', 'head'), may hold values from -450 to 450
- merge_weight: bfloat16 [3, 2880, 2880], P(None, 'head', 'segment'), may hold values from -0.0625 to 0.0625
- query_weight: bfloat16 [5760, 2048], P('ctx', ('segment', 'head')), may hold values from -1 to 1
- key_weight: bfloat16 [5760, 256], P('ctx', 'segment'), may hold values from -8 to 8
- value_weight: bfloat16 [5760, 256], P('ctx', 'segment'), may hold values from -0.078125 to 0.078125
- block_order: int32 [64], replicated, may hold values from 0 to 63, each once
Outputs:
- attended: bfloat16 [8192, 2048], P('ctx', ('segment', 'head'))
Inputs may be any that keep to these rules, and one draw needn't show every extreme that they name: `block_order`: a permutation of the sequence blocks.
All inputs are finite; a program needn't handle non-finite values.
Results may differ from a plain program's by a relative error of at most 0.023.
The roundings to bfloat16 on the way count: a program that leaves them out, or rounds other values in their place, can miss the bound.
Values may be sent and summed in bfloat16 or wider, within the bound.
No kernel may reach another device: no remote copies, remote signals or barrier semaphores. Data moves between devices by JAX's collectives and lax.ppermute only.
A program may use at most 64 MiB of HBM per device.

v0:
```python
import math
import jax
import jax.numpy as jnp
from jax import lax
from jax.sharding import PartitionSpec as P

HD = 64


def normalize(matrix):
    widened = matrix.astype(jnp.float32)
    return widened * lax.rsqrt(jnp.mean(widened * widened, axis=-1, keepdims=True) + 1e-06)


def seq_positions(row_ids, order, block_len):
    block_ids = jnp.arange(order.shape[0], dtype=jnp.int32)
    matches = (row_ids // block_len)[:, None] == block_ids[None, :]
    block_first = jnp.sum(jnp.where(matches, order[None, :], 0), axis=1)
    return block_first * block_len + row_ids % block_len


def attend_block(carry, query_heads, query_pos, key_blk, value_blk, key_pos):
    run_max, run_total, accum = carry
    tok_rows, heads_count, head_size = query_heads.shape
    scores = (
        jnp.einsum("tgd,nd->tgn", query_heads, key_blk, preferred_element_type=jnp.float32) * 0.125
    )
    allowed = key_pos[None, None, :] <= query_pos[:, None, None]
    scores = jnp.where(allowed, scores, -1e30)
    new_max = jnp.maximum(run_max, jnp.max(scores, axis=2))
    rescale = jnp.exp(run_max - new_max)
    unscaled = jnp.where(allowed, jnp.exp(scores - new_max[:, :, None]), 0.0)
    run_total = run_total * rescale + jnp.sum(unscaled, axis=2)
    mixed_rows = jnp.einsum(
        "tgn,nd->tgd", unscaled.astype(jnp.bfloat16), value_blk, preferred_element_type=jnp.float32
    )
    grown = accum.reshape(tok_rows, heads_count, head_size) * rescale[:, :, None] + mixed_rows
    return (new_max, run_total, grown.reshape(tok_rows, heads_count * head_size))


def body(hidden, merge_weight, query_weight, key_weight, value_weight, block_order):
    tok_rows = hidden.shape[1]
    block_len = tok_rows // 2
    segments = lax.axis_size("segment")
    heads_here = lax.axis_size("head")
    segment_id = lax.axis_index("segment")
    head_id = lax.axis_index("head")
    ctx_id = lax.axis_index("ctx")
    sections = lax.all_gather(hidden, "segment", axis=0, tiled=True)
    partial_value = jnp.einsum(
        "ktf,kfc->tc", sections[:3], merge_weight, preferred_element_type=jnp.float32
    )
    col_piece = partial_value.shape[1] // heads_here
    summed = lax.psum(partial_value, "head")
    merged_part = lax.dynamic_slice_in_dim(summed, head_id * col_piece, col_piece, 1)
    merged_part = merged_part.astype(jnp.bfloat16)
    embed_part = lax.dynamic_slice_in_dim(sections[3], segment_id * col_piece, col_piece, 1)
    merged_all, embed_mixed = (
        lax.all_gather(merged_part, ("segment", "head"), axis=1, tiled=True),
        lax.all_gather(embed_part, ("segment", "head"), axis=1, tiled=True),
    )
    embed_all = embed_mixed.reshape(tok_rows, segments, heads_here, col_piece).transpose(0, 2, 1, 3)
    embed_all = embed_all.reshape(tok_rows, segments * heads_here * col_piece)
    draft_input = jnp.concatenate([normalize(embed_all), normalize(merged_all)], axis=1).astype(
        jnp.bfloat16
    )
    query_piece = lax.all_gather(query_weight, "ctx", axis=0, tiled=True)
    key_piece = lax.all_gather(key_weight, "ctx", axis=0, tiled=True)
    value_piece = lax.all_gather(value_weight, "ctx", axis=0, tiled=True)
    query_acc = jnp.dot(draft_input, query_piece, preferred_element_type=jnp.float32)
    key_acc = jnp.dot(draft_input, key_piece, preferred_element_type=jnp.float32)
    value_acc = jnp.dot(draft_input, value_piece, preferred_element_type=jnp.float32)
    query_acc, key_acc, value_acc = (query_acc, key_acc, value_acc)
    query_heads = query_acc.astype(jnp.bfloat16).reshape(tok_rows, -1, HD)
    key_vectors = key_acc.astype(jnp.bfloat16)
    value_vectors = value_acc.astype(jnp.bfloat16)
    heads_count = query_heads.shape[1]
    query_pos = seq_positions(
        ctx_id * tok_rows + jnp.arange(tok_rows, dtype=jnp.int32), block_order, block_len
    )
    initial_attn = (
        jnp.full((tok_rows, heads_count), -1e30, jnp.float32),
        jnp.zeros((tok_rows, heads_count), jnp.float32),
        jnp.zeros((tok_rows, heads_count * HD), jnp.float32),
    )
    key_piece = lax.all_gather(key_vectors, "ctx", axis=0, tiled=True)
    value_piece = lax.all_gather(value_vectors, "ctx", axis=0, tiled=True)
    row_count = key_piece.shape[0]
    key_step = math.gcd(row_count, 512)

    def one_block(turn_index, carried):
        offset = turn_index * key_step
        key_blk = lax.dynamic_slice_in_dim(key_piece, offset, key_step, 0)
        value_blk = lax.dynamic_slice_in_dim(value_piece, offset, key_step, 0)
        key_pos = seq_positions(
            offset + jnp.arange(key_step, dtype=jnp.int32), block_order, block_len
        )
        return attend_block(carried, query_heads, query_pos, key_blk, value_blk, key_pos)

    run_max, run_total, accum = lax.fori_loop(0, row_count // key_step, one_block, initial_attn)
    output = accum.reshape(tok_rows, heads_count, HD) / run_total[:, :, None]
    return output.reshape(tok_rows, heads_count * HD).astype(jnp.bfloat16)


def solution(mesh):
    return jax.shard_map(
        body,
        mesh=mesh,
        in_specs=(
            P("segment", "ctx", "head"),
            P(None, "head", "segment"),
            P("ctx", ("segment", "head")),
            P("ctx", "segment"),
            P("ctx", "segment"),
            P(),
        ),
        out_specs=P("ctx", ("segment", "head")),
        check_vma=False,
    )
```

profile of v0, /device:TPU:4, one launch (start us, length us, event | category | flops | bytes accessed | tf_op | source)
XLA Modules:
  0.0 691.7 jit_solution(7909298819602587909)
XLA Ops:
  7.3 38.2 %all-gather.12.cloned.1.call-done = bf16[4,256,720]{1,2,0:T(8,128)(2,1)} async-done(((bf16[1,256,720]{1,2,0:T(8,128)(2,1)}), bf16[4,256,720]{1,2,0:T(8,128)(2,1)}) %all-gather.12.cloned.1.call-update) | async-done | bytes 1474576 | tf_op jit(solution)/shard_map/all_gather | solution.py:49
  47.5 3.6 convolution_bitcast_fusion
  51.1 25.7 %all-reduce.1 = bf16[256,720]{0,1:T(8,128)(2,1)} all-reduce(f32[256,720]{0,1:T(8,128)} %convolution_bitcast_fusion), channel_id=1, replica_groups=mesh['segment'=4,'ctx'=32,'head'=4] {'head'}, use_global_device_ids=true, to_apply=%region_1.0 | all-reduce | flops 184320 | bytes 1105920 | tf_op jit(solution)/shard_map/psum | solution.py:54
  76.8 1.5 fusion.23
  79.0 83.5 %all-gather.4 = bf16[32,180,64]{1,2,0:T(8,128)(2,1)S(1)} all-gather(bf16[1,180,64]{1,2,0:T(8,128)(2,1)S(1)} %bitcast.59), channel_id=1, replica_groups=mesh['segment'=4,'ctx'=32,'head'=4] {'ctx'}, dimensions={0}, use_global_device_ids=true | all-gather | bytes 760320 | tf_op jit(solution)/shard_map/all_gather | solution.py:69
  162.5 1.6 copy.29
  164.1 3.1 reshape.158
  167.2 31.9 %multiply_reduce_fusion.1 = (f32[256]{0:T(256)S(1)}, f32[256,2880]{0,1:T(8,128)}) fusion(bf16[1,256,2880]{1,0,2:T(2,128)(2,1)} %all-gather.18.cloned.1.call-done), kind=kLoop, calls=%fused_computation.39 | loop fusion | flops 2211584 | bytes 4424704 | tf_op jit(solution)/shard_map/reduce_sum | solution.py:12
  199.1 4.0 reshape.145
  203.2 3.8 copy.26
  207.0 4.1 reshape.144
  211.1 3.4 reshape.159
  214.5 2.4 multiply_reduce_fusion
  222.4 78.1 %all-gather.2 = bf16[32,180,64]{1,2,0:T(8,128)(2,1)S(1)} all-gather(bf16[1,180,64]{1,2,0:T(8,128)(2,1)S(1)} %bitcast.60), channel_id=1, replica_groups=mesh['segment'=4,'ctx'=32,'head'=4] {'ctx'}, dimensions={0}, use_global_device_ids=true | all-gather | bytes 760320 | tf_op jit(solution)/shard_map/all_gather | solution.py:68
  300.5 1.6 copy.28
  302.0 3.2 reshape.154
  305.2 3.3 convolution_convert_fusion.2
  308.7 9.7 %all-gather.22.cloned.1.call-done = bf16[32,180,128]{2,1,0:T(8,128)(2,1)} async-done(((bf16[1,180,128]{2,1,0:T(8,128)(2,1)}), bf16[32,180,128]{2,1,0:T(8,128)(2,1)}) %all-gather.22.cloned.1.call-update) | async-done | bytes 1474576 | tf_op jit(solution)/shard_map/all_gather | solution.py:67
  318.4 3.3 reshape.156
  321.7 3.0 convolution_convert_fusion
  324.7 127.4 %all-gather.16.cloned.1.call-done = bf16[8192,64]{0,1:T(8,128)(2,1)} async-done(((bf16[256,64]{0,1:T(8,128)(2,1)}), bf16[8192,64]{0,1:T(8,128)(2,1)}) %all-gather.16.cloned.1.call-update) | async-done | bytes 1048592 | tf_op jit(solution)/shard_map/all_gather | solution.py:87
  452.1 132.5 %all-gather.14.cloned.1.call-done = bf16[8192,64]{0,1:T(8,128)(2,1)} async-done(((bf16[256,64]{0,1:T(8,128)(2,1)}), bf16[8192,64]{0,1:T(8,128)(2,1)}) %all-gather.14.cloned.1.call-update) | async-done | bytes 1048592 | tf_op jit(solution)/shard_map/all_gather | solution.py:86
  585.3 98.0 %while.20 = (s32[]{:T(128)}, f32[256,2]{0,1:T(2,128)S(1)}, f32[256,2]{0,1:T(2,128)S(1)}, f32[256,128]{0,1:T(8,128)}, s32[64]{0:T(128)S(1)}, /*index=5*/s32[256]{...) while((s32[]{:T(128)}, f32[256,2]{0,1:T(2,128)S(1)}, ...), condition=%wide.region_8.9_spmd.clone, body=%wide.region_4.8_spmd.clone.sunk | while | flops 69780480 | bytes 4175302 | solution.py:100
  585.6 2.2 fusion.48
  587.7 1.4 fusion.50
  589.2 2.2 convolution_add_fusion.2
  591.7 2.2 fusion.48
  593.8 1.4 fusion.50
  595.3 2.2 convolution_add_fusion.2
  597.8 2.2 fusion.48
  600.0 1.4 fusion.50
  601.4 2.2 convolution_add_fusion.2
  603.9 2.2 fusion.48
  606.1 1.4 fusion.50
  607.6 2.2 convolution_add_fusion.2
  610.1 2.2 fusion.48
  612.2 1.4 fusion.50
  613.7 2.2 convolution_add_fusion.2
  616.2 2.2 fusion.48
  618.3 1.4 fusion.50
  619.8 2.2 convolution_add_fusion.2
  622.3 2.2 fusion.48
  624.5 1.4 fusion.50
  625.9 2.2 convolution_add_fusion.2
  628.4 2.2 fusion.48
  630.6 1.4 fusion.50
  632.1 2.2 convolution_add_fusion.2
  634.5 2.2 fusion.48
  636.7 1.4 fusion.50
  638.2 2.2 convolution_add_fusion.2
  640.7 2.2 fusion.48
  644.3 2.2 convolution_add_fusion.2
  646.8 2.2 fusion.48
  650.4 2.2 convolution_add_fusion.2
  652.9 2.2 fusion.48
  656.5 2.2 convolution_add_fusion.2
  659.0 2.2 fusion.48
  662.7 2.2 convolution_add_fusion.2
  665.1 2.2 fusion.48
  668.8 2.2 convolution_add_fusion.2
  671.3 2.2 fusion.48
  674.9 2.2 convolution_add_fusion.2
  677.4 2.2 fusion.48
  681.0 2.2 convolution_add_fusion.2
  (167 shorter events, 26.0 us)
Async XLA Ops:
  6.5 41.0 %copy-start = (bf16[3,720,720]{2,1,0:T(8,128)(2,1)S(1)}, bf16[3,720,720]{2,1,0:T(8,128)(2,1)}, u32[]{:S(2)}) copy-start(bf16[3,720,720]{2,1,0:T(8,128)(2,1)} %param.9) | copy-start | bytes 9331204
  6.5 39.0 %all-gather.12.cloned.1.call-start = ((), (), s32[]{:S(2)}) async-start(), calls=%async_computation | async-start | bytes 1843200 | tf_op jit(solution)/shard_map/all_gather | solution.py:49
  7.3 160.0 %all-gather.18.cloned.1.call-start = ((), (), s32[]{:S(2)}) async-start(), calls=%async_computation.3 | async-start | bytes 3133440 | tf_op jit(solution)/shard_map/all_gather | solution.py:60
  47.4 163.6 %all-gather.20.cloned.1.call-start = ((), (), s32[]{:S(2)}) async-start(), calls=%async_computation.4 | async-start | bytes 1601536 | tf_op jit(solution)/shard_map/all_gather | solution.py:59
  47.5 31.5 %copy-start.6 = (bf16[180,64]{0,1:T(8,128)(2,1)S(1)}, bf16[180,64]{0,1:T(8,128)(2,1)}, u32[]{:S(2)}) copy-start(bf16[180,64]{0,1:T(8,128)(2,1)} %param.12) | copy-start | bytes 69124
  78.3 240.1 %all-gather.22.cloned.1.call-start = ((), (), s32[]{:S(2)}) async-start(), calls=%async_computation.5 | async-start | bytes 1554432 | tf_op jit(solution)/shard_map/all_gather | solution.py:67
  78.9 373.2 %all-gather.16.cloned.1.call-start = ((), (), s32[]{:S(2)}) async-start(), calls=%async_computation.2 | async-start | bytes 1081344 | tf_op jit(solution)/shard_map/all_gather | solution.py:87
  214.5 2.7 copy-start.1
  216.9 1.9 copy-start.2
  218.8 1.1 copy-start.3
  218.8 2.2 copy-start.5
  219.9 1.1 copy-start.4
  221.0 1.3 copy-start.7
  222.3 362.3 %all-gather.14.cloned.1.call-start = ((), (), s32[]{:S(2)}) async-start(), calls=%async_computation.1 | async-start | bytes 1081344 | tf_op jit(solution)/shard_map/all_gather | solution.py:86
  305.2 3.4 copy-start.8
Sparse Core Ops, SparseCore 0:
  9.5 36.0 all-gather.11
  47.6 58.5 all-gather.17
  108.3 56.1 all-gather.19
  167.5 150.8 all-gather.21
  321.1 130.8 all-gather.15
  454.9 129.7 all-gather.13
where the time goes:
time: 694 us; the launch traced here: 692 us
  waiting for transfers between devices  309 us (45%)
  blocking collectives  187 us (27%)
  matrix products  81 us (12%)
  other arithmetic  63.7 us (9%)
  local copies, waits for them, and re-layouts  36.5 us (5%)
  between operations  13.6 us (2%)
    all_gather x1, waiting for transfers between devices, body(): key_piece = lax.all_gather(key_vectors, 'ctx', axis=0, tiled=True)  133 us
    all_gather x1, waiting for transfers between devices, body(): value_piece = lax.all_gather(value_vectors, 'ctx', axis=0, tiled=True)  127 us
    all_gather x1, blocking collectives, body(): value_piece = lax.all_gather(value_weight, 'ctx', axis=0, tiled=True)  83.5 us
    all_gather x1, blocking collectives, body(): key_piece = lax.all_gather(key_weight, 'ctx', axis=0, tiled=True)  78.1 us
    all_gather x1, waiting for transfers between devices, body(): sections = lax.all_gather(hidden, 'segment', axis=0, tiled=True)  38.2 us
    dot_general x16, matrix products, attend_block(): jnp.einsum('tgn,nd->tgd', unscaled.astype(jnp.bfloat16), value_blk, prefe...  35.4 us
    dot_general x16, matrix products, attend_block(): jnp.einsum('tgd,nd->tgn', query_heads, key_blk, preferred_element_type=jn...  34.5 us
    reduce_sum x2, other arithmetic, normalize(): jnp.mean(widened * widened, axis=-1, keepdims=True) + 1e-06  34.3 us
  transfers between devices with their start and end apart: 6, of which 4 were waited for; matrix products, arithmetic and copies ran while one was open for 11% of the time, Pallas kernels for 0%

commit v1 on v0

--- a/solution.py
+++ b/solution.py
@@ -51,7 +51,7 @@
         "ktf,kfc->tc", sections[:3], merge_weight, preferred_element_type=jnp.float32
     )
     col_piece = partial_value.shape[1] // heads_here
-    summed = lax.psum(partial_value, "head")
+    summed = jnp.sum(lax.all_gather(partial_value, "head"), axis=0)
     merged_part = lax.dynamic_slice_in_dim(summed, head_id * col_piece, col_piece, 1)
     merged_part = merged_part.astype(jnp.bfloat16)
     embed_part = lax.dynamic_slice_in_dim(sections[3], segment_id * col_piece, col_piece, 1)

time: 694 us -> 741 us (1.068)
  waiting for transfers between devices: 309 us -> 373 us
  blocking collectives: 187 us -> 160 us
    all_gather x0 -> x1, waiting for transfers between devices: none -> 43.7 us  [body(): summed = jnp.sum(lax.all_gather(partial_value, 'head'), axis=0)]
    psum x1 -> x0, blocking collectives: 25.7 us -> none  [body(): summed = lax.psum(partial_value, 'head')]
    all_gather x1, waiting for transfers between devices: 9.71 us -> 30.9 us  [body(): query_piece = lax.all_gather(query_weight, 'ctx', axis=0, tiled=True)]
  transfers between devices with their start and end apart: 6 -> 7, of which waited for: 4 -> 5; matrix products, arithmetic and copies ran while one was open for 11% -> 12% of each run, Pallas kernels for 0% -> 0%
where the time goes in v1:
time: 741 us; the launch traced here: 738 us
  waiting for transfers between devices  373 us (50%)
  blocking collectives  160 us (22%)
  matrix products  80.8 us (11%)
  other arithmetic  71 us (10%)
  local copies, waits for them, and re-layouts  39.3 us (5%)
  between operations  13.6 us (2%)
    all_gather x1, waiting for transfers between devices, body(): key_piece = lax.all_gather(key_vectors, 'ctx', axis=0, tiled=True)  133 us
    all_gather x1, waiting for transfers between devices, body(): value_piece = lax.all_gather(value_vectors, 'ctx', axis=0, tiled=True)  126 us
    all_gather x1, blocking collectives, body(): value_piece = lax.all_gather(value_weight, 'ctx', axis=0, tiled=True)  82.7 us
    all_gather x1, blocking collectives, body(): key_piece = lax.all_gather(key_weight, 'ctx', axis=0, tiled=True)  77.4 us
    all_gather x1, waiting for transfers between devices, body(): summed = jnp.sum(lax.all_gather(partial_value, 'head'), axis=0)  43.7 us
    all_gather x1, waiting for transfers between devices, body(): sections = lax.all_gather(hidden, 'segment', axis=0, tiled=True)  38.2 us
    dot_general x16, matrix products, attend_block(): jnp.einsum('tgn,nd->tgd', unscaled.astype(jnp.bfloat16), value_blk, prefe...  35.6 us
    reduce_sum x2, other arithmetic, normalize(): jnp.mean(widened * widened, axis=-1, keepdims=True) + 1e-06  34.3 us
  transfers between devices with their start and end apart: 7, of which 5 were waited for; matrix products, arithmetic and copies ran while one was open for 12% of the time, Pallas kernels for 0%

profile of v1, /device:TPU:4, one launch (start us, length us, event | category | flops | bytes accessed | tf_op | source)
XLA Modules:
  0.0 738.5 jit_solution(6835021973550704962)
XLA Ops:
  7.3 38.2 %all-gather.14.cloned.1.call-done = bf16[4,256,720]{1,2,0:T(8,128)(2,1)} async-done(((bf16[1,256,720]{1,2,0:T(8,128)(2,1)}), bf16[4,256,720]{1,2,0:T(8,128)(2,1)}) %all-gather.14.cloned.1.call-update) | async-done | bytes 1474576 | tf_op jit(solution)/shard_map/all_gather | solution.py:49
  45.5 3.5 convolution_bitcast_fusion
  51.1 43.7 %all-gather.22.cloned.1.call-done = f32[1024,720]{0,1:T(8,128)} async-done(((f32[256,720]{0,1:T(8,128)}), f32[1024,720]{0,1:T(8,128)}) %all-gather.22.cloned.1.call-update) | async-done | bytes 2949136 | tf_op jit(solution)/shard_map/all_gather | solution.py:54
  94.8 4.9 reshape.147
  99.7 4.4 reduce_sum.70
  104.0 1.5 fusion.23
  106.3 82.7 %all-gather.5 = bf16[32,180,64]{1,2,0:T(8,128)(2,1)S(1)} all-gather(bf16[1,180,64]{1,2,0:T(8,128)(2,1)S(1)} %bitcast.61), channel_id=1, replica_groups=mesh['segment'=4,'ctx'=32,'head'=4] {'ctx'}, dimensions={0}, use_global_device_ids=true | all-gather | bytes 760320 | tf_op jit(solution)/shard_map/all_gather | solution.py:69
  189.0 1.6 copy.29
  190.5 3.1 reshape.159
  193.7 31.9 %multiply_reduce_fusion.1 = (f32[256]{0:T(256)S(1)}, f32[256,2880]{0,1:T(8,128)}) fusion(bf16[1,256,2880]{1,0,2:T(2,128)(2,1)} %all-gather.20.cloned.1.call-done), kind=kLoop, calls=%fused_computation.39 | loop fusion | flops 2211584 | bytes 4424704 | tf_op jit(solution)/shard_map/reduce_sum | solution.py:12
  225.6 4.0 reshape.145
  229.6 3.8 copy.26
  233.4 4.1 reshape.144
  237.5 3.2 multiply_convert_fusion.1
  240.7 3.4 reshape.160
  244.1 2.4 multiply_reduce_fusion
  249.6 77.4 %all-gather.3 = bf16[32,180,64]{1,2,0:T(8,128)(2,1)S(1)} all-gather(bf16[1,180,64]{1,2,0:T(8,128)(2,1)S(1)} %bitcast.62), channel_id=1, replica_groups=mesh['segment'=4,'ctx'=32,'head'=4] {'ctx'}, dimensions={0}, use_global_device_ids=true | all-gather | bytes 760320 | tf_op jit(solution)/shard_map/all_gather | solution.py:68
  327.0 1.5 copy.28
  328.5 3.2 reshape.155
  331.7 3.3 convolution_convert_fusion.2
  335.2 30.9 %all-gather.26.cloned.1.call-done = bf16[32,180,128]{2,1,0:T(8,128)(2,1)} async-done(((bf16[1,180,128]{2,1,0:T(8,128)(2,1)}), bf16[32,180,128]{2,1,0:T(8,128)(2,1)}) %all-gather.26.cloned.1.call-update) | async-done | bytes 1474576 | tf_op jit(solution)/shard_map/all_gather | solution.py:67
  366.1 3.3 reshape.157
  369.4 3.0 convolution_convert_fusion
  372.4 126.4 %all-gather.18.cloned.1.call-done = bf16[8192,64]{0,1:T(8,128)(2,1)} async-done(((bf16[256,64]{0,1:T(8,128)(2,1)}), bf16[8192,64]{0,1:T(8,128)(2,1)}) %all-gather.18.cloned.1.call-update) | async-done | bytes 1048592 | tf_op jit(solution)/shard_map/all_gather | solution.py:87
  498.8 132.7 %all-gather.16.cloned.1.call-done = bf16[8192,64]{0,1:T(8,128)(2,1)} async-done(((bf16[256,64]{0,1:T(8,128)(2,1)}), bf16[8192,64]{0,1:T(8,128)(2,1)}) %all-gather.16.cloned.1.call-update) | async-done | bytes 1048592 | tf_op jit(solution)/shard_map/all_gather | solution.py:86
  632.2 97.8 %while.20 = (s32[]{:T(128)}, f32[256,2]{0,1:T(2,128)S(1)}, f32[256,2]{0,1:T(2,128)S(1)}, f32[256,128]{0,1:T(8,128)}, s32[64]{0:T(128)S(1)}, /*index=5*/s32[256]{...) while((s32[]{:T(128)}, f32[256,2]{0,1:T(2,128)S(1)}, ...), condition=%wide.region_8.9_spmd.clone, body=%wide.region_4.8_spmd.clone.sunk | while | flops 69780480 | bytes 4175302 | solution.py:100
  632.4 2.1 fusion.48
  634.6 1.4 fusion.50
  636.0 2.2 convolution_add_fusion.2
  638.5 2.1 fusion.48
  640.7 1.4 fusion.50
  642.1 2.2 convolution_add_fusion.2
  644.6 2.1 fusion.48
  646.8 1.4 fusion.50
  648.3 2.2 convolution_add_fusion.2
  650.8 2.1 fusion.48
  652.9 1.4 fusion.50
  654.4 2.2 convolution_add_fusion.2
  656.9 2.1 fusion.48
  659.0 1.4 fusion.50
  660.5 2.2 convolution_add_fusion.2
  663.0 2.1 fusion.48
  665.1 1.4 fusion.50
  666.6 2.2 convolution_add_fusion.2
  669.1 2.1 fusion.48
  672.7 2.2 convolution_add_fusion.2
  675.2 2.1 fusion.48
  678.8 2.2 convolution_add_fusion.2
  681.3 2.1 fusion.48
  684.9 2.2 convolution_add_fusion.2
  687.4 2.1 fusion.48
  691.1 2.2 convolution_add_fusion.2
  693.6 2.1 fusion.48
  697.2 2.2 convolution_add_fusion.2
  699.7 2.1 fusion.48
  703.3 2.2 convolution_add_fusion.2
  705.8 2.1 fusion.48
  709.4 2.2 convolution_add_fusion.2
  711.9 2.1 fusion.48
  715.5 2.2 convolution_add_fusion.2
  718.0 2.1 fusion.48
  721.6 2.2 convolution_add_fusion.2
  724.1 2.1 fusion.48
  727.7 2.2 convolution_add_fusion.2
  (169 shorter events, 28.1 us)
Async XLA Ops:
  6.5 39.0 %copy-start = (bf16[3,720,720]{2,1,0:T(8,128)(2,1)S(1)}, bf16[3,720,720]{2,1,0:T(8,128)(2,1)}, u32[]{:S(2)}) copy-start(bf16[3,720,720]{2,1,0:T(8,128)(2,1)} %param.9) | copy-start | bytes 9331204
  6.5 39.0 %all-gather.14.cloned.1.call-start = ((), (), s32[]{:S(2)}) async-start(), calls=%async_computation | async-start | bytes 1843200 | tf_op jit(solution)/shard_map/all_gather | solution.py:49
  7.3 87.5 %all-gather.22.cloned.1.call-start = ((), (), s32[]{:S(2)}) async-start(), calls=%async_computation.4 | async-start | bytes 3686400 | tf_op jit(solution)/shard_map/all_gather | solution.py:54
  49.1 144.6 %all-gather.20.cloned.1.call-start = ((), (), s32[]{:S(2)}) async-start(), calls=%async_computation.3 | async-start | bytes 3133440 | tf_op jit(solution)/shard_map/all_gather | solution.py:60
  51.1 189.6 %all-gather.24.cloned.1.call-start = ((), (), s32[]{:S(2)}) async-start(), calls=%async_computation.5 | async-start | bytes 1601536 | tf_op jit(solution)/shard_map/all_gather | solution.py:59
  99.7 6.6 copy-start.5
  105.6 260.5 %all-gather.26.cloned.1.call-start = ((), (), s32[]{:S(2)}) async-start(), calls=%async_computation.6 | async-start | bytes 1554432 | tf_op jit(solution)/shard_map/all_gather | solution.py:67
  106.2 392.6 %all-gather.18.cloned.1.call-start = ((), (), s32[]{:S(2)}) async-start(), calls=%async_computation.2 | async-start | bytes 1081344 | tf_op jit(solution)/shard_map/all_gather | solution.py:87
  244.1 2.7 copy-start.1
  246.5 1.7 copy-start.2
  246.5 1.8 copy-start.4
  247.0 1.2 copy-start.3
  248.3 1.3 copy-start.6
  249.5 382.0 %all-gather.16.cloned.1.call-start = ((), (), s32[]{:S(2)}) async-start(), calls=%async_computation.1 | async-start | bytes 1081344 | tf_op jit(solution)/shard_map/all_gather | solution.py:86
  331.7 3.4 copy-start.7
Sparse Core Ops, SparseCore 0:
  9.5 36.0 all-gather.13
  49.2 45.5 all-gather.21
  96.9 58.1 all-gather.19
  157.1 57.1 all-gather.23
  217.3 148.7 all-gather.25
  368.8 129.9 all-gather.17
  501.7 129.7 all-gather.15
